TPU v7x, 256 devices: a whole 4x4x8 slice. The times are simulated.
256 devices in a mesh: blk: 128 (over x, z, y_lo, core), rep: 2 (over y_hi).
Axes of the slice: x: 4, y: 4 (y_hi: 2, y_lo: 2; y = y_hi * 2 + y_lo), z: 8, core: 2. Of those that a mesh axis runs over, the one named last changes fastest.
Arguments:
- image_emb: bfloat16 [131072, 1152], P(('blk', 'rep')), may hold values from -0.19921875 to 0.19921875
- text_emb: bfloat16 [131072, 1152], P(('blk', 'rep')), may hold values from -0.19921875 to 0.19921875
- log_temp: float32 [], replicated, may hold values from 1 to 2
- bias: float32 [], replicated, may hold values from -2 to 0
Outputs:
- row_loss: float32 [131072], P(('blk', 'rep'))
- grad_image: float32 [131072, 1152], P(('blk', 'rep'))
- grad_text: float32 [131072, 1152], P(('blk', 'rep'))
All inputs are finite; a program needn't handle non-finite values.
Results may differ from a plain program's by a relative error of at most 0.0042.
Values may be sent and summed in bfloat16 or wider, within the bound.
No kernel may reach another device: no remote copies, remote signals or barrier semaphores. Data moves between devices by JAX's collectives and lax.ppermute only.
A program may use at most 64 MiB of HBM per device.

v0:
```python
import jax
import jax.numpy as jnp
from jax import lax
from jax.sharding import PartitionSpec as P

STEPS = 4


EPSILON = 1e-06


def shifted(x, axis, by):
    count = lax.axis_size(axis)
    return lax.ppermute(x, axis, [(i, (i + by) % count) for i in range(count)])


def unit_rows(embedding):
    values = embedding.astype(jnp.float32)
    scale = lax.rsqrt(jnp.sum(values * values, axis=-1, keepdims=True) + EPSILON)
    return (values * scale, scale)


def block_weights(image_low, partner, temper, bias, labels):
    logits = (
        temper
        * lax.dot_general(
            image_low, partner, (((1,), (1,)), ((), ())), preferred_element_type=jnp.float32
        )
        + bias
    )
    losses = -jnp.sum(jax.nn.log_sigmoid(labels * logits), axis=-1)
    weights = (-labels * jax.nn.sigmoid(-labels * logits) * temper).astype(jnp.bfloat16)
    return (losses, weights)


def block_terms(image_low, partner, temper, bias, labels):
    losses, weights = block_weights(image_low, partner, temper, bias, labels)
    grad_img = jnp.dot(weights, partner, preferred_element_type=jnp.float32)
    grad_txt = lax.dot_general(
        weights, image_low, (((0,), (0,)), ((), ())), preferred_element_type=jnp.float32
    )
    return (losses, grad_img, grad_txt)


def unit_backward(unit, scale, grad_unit):
    return scale * (grad_unit - unit * jnp.sum(unit * grad_unit, axis=-1, keepdims=True))


def body(image_emb, text_emb, log_temp, bias):
    row_count = image_emb.shape[0]
    image_unit, image_scale = unit_rows(image_emb)
    text_unit, text_scale = unit_rows(text_emb)
    image_low = image_unit.astype(jnp.bfloat16)
    text_low = text_unit.astype(jnp.bfloat16)
    temper = jnp.exp(log_temp)
    positive = 2.0 * jnp.eye(row_count, dtype=jnp.float32) - 1.0
    negative = -jnp.ones((row_count, row_count), jnp.float32)
    losses = jnp.zeros((row_count,), jnp.float32)
    grad_img = jnp.zeros(image_unit.shape, jnp.float32)
    partner = text_low
    carried = jnp.zeros(text_unit.shape, jnp.float32)
    for offset in range(STEPS):
        if offset > 0:
            partner = shifted(partner, ("blk", "rep"), 1)
            carried = shifted(carried, ("blk", "rep"), 1)
        labels = positive if offset == 0 else negative
        step_loss, step_img, step_txt = block_terms(image_low, partner, temper, bias, labels)
        losses = losses + step_loss
        grad_img = grad_img + step_img
        carried = carried + step_txt
    grad_txt = shifted(carried, ("blk", "rep"), 1 - STEPS)
    grad_image = unit_backward(image_unit, image_scale, grad_img)
    grad_text = unit_backward(text_unit, text_scale, grad_txt)
    return (losses, grad_image, grad_text)


def solution(mesh):
    return jax.shard_map(
        body,
        mesh=mesh,
        in_specs=(P(("blk", "rep"), None), P(("blk", "rep"), None), P(), P()),
        out_specs=(P(("blk", "rep")), P(("blk", "rep"), None), P(("blk", "rep"), None)),
        check_vma=False,
    )
```

profile of v0, /device:TPU:0, one launch (start us, length us, event | category | flops | bytes accessed | tf_op | source)
XLA Modules:
  0.0 312.6 jit_solution(15883365958330631953)
XLA Ops:
  1.4 1.6 fusion.13
  3.0 1.5 fusion.2
  5.5 1.5 fusion.18
  7.1 1.1 fusion.24
  8.2 1.5 collective-permute-start.3
  9.8 75.7 %collective-permute-done = bf16[512,1152]{1,0:T(8,128)(2,1)S(1)} collective-permute-done((bf16[512,1152]{1,0:T(8,128)(2,1)S(1)}, bf16[512,1152]{1,0:T(8,128)(2,1)S(1)}, u32[]{:S(2)}, u32[]{:S(2)}) %collective-permute-start) | collective-permute-done | bytes 1179680 | tf_op jit(solution)/shard_map/ppermute | solution.py:14
  85.5 1.5 fusion.19
  87.0 1.0 convolution_add_fusion
  88.1 4.1 %collective-permute-start.4 = (f32[512,1152]{1,0:T(8,128)S(1)}, f32[512,1152]{1,0:T(8,128)S(1)}, u32[]{:S(2)}, u32[]{:S(2)}) collective-permute-start(f32[512,1152]{1,0:T(8,128)S(1)} %convolution_add_fusion), channel_id=1, source_target_pairs={{0,1},{1,2},{2,3},{3,4},{4,5},{5,6},{6,7},{7,8},{8,9},{9,10},{10,1... | collective-permute-start | bytes 7077896 | tf_op jit(solution)/shard_map/ppermute | solution.py:14
  92.7 74.3 %collective-permute-done.1 = bf16[512,1152]{1,0:T(8,128)(2,1)S(1)} collective-permute-done((bf16[512,1152]{1,0:T(8,128)(2,1)S(1)}, bf16[512,1152]{1,0:T(8,128)(2,1)S(1)}, u32[]{:S(2)}, u32[]{:S(2)}) %collective-permute-start.1) | collective-permute-done | bytes 1179680 | tf_op jit(solution)/shard_map/ppermute | solution.py:14
  167.1 1.5 fusion.20
  168.6 1.1 fusion.22
  169.9 4.3 %collective-permute-start.5 = (f32[512,1152]{1,0:T(8,128)S(1)}, f32[512,1152]{1,0:T(8,128)S(1)}, u32[]{:S(2)}, u32[]{:S(2)}) collective-permute-start(f32[512,1152]{1,0:T(8,128)S(1)} %add.110), channel_id=1, source_target_pairs={{0,1},{1,2},{2,3},{3,4},{4,5},{5,6},{6,7},{7,8},{8,9},{9,10},{10,1... | collective-permute-start | bytes 7077896 | tf_op jit(solution)/shard_map/ppermute | solution.py:14
  174.2 2.0 collective-permute-start.2
  176.2 73.1 %collective-permute-done.2 = bf16[512,1152]{1,0:T(8,128)(2,1)S(1)} collective-permute-done((bf16[512,1152]{1,0:T(8,128)(2,1)S(1)}, bf16[512,1152]{1,0:T(8,128)(2,1)S(1)}, u32[]{:S(2)}, u32[]{:S(2)}) %collective-permute-start.2) | collective-permute-done | bytes 1179680 | tf_op jit(solution)/shard_map/ppermute | solution.py:14
  249.3 1.5 fusion.21
  250.8 1.1 fusion.23
  252.2 10.3 %collective-permute-start.6 = (f32[512,1152]{1,0:T(8,128)S(1)}, f32[512,1152]{1,0:T(8,128)S(1)}, u32[]{:S(2)}, u32[]{:S(2)}) collective-permute-start(f32[512,1152]{1,0:T(8,128)S(1)} %add.111), channel_id=1, source_target_pairs={{0,253},{1,254},{2,255},{3,0},{4,1},{5,2},{6,3},{7,4},{8,5},{9,6},... | collective-permute-start | bytes 7077896 | tf_op jit(solution)/shard_map/ppermute | solution.py:14
  262.4 0.9 fusion.25
  264.3 0.9 convolution_add_fusion.2
  265.8 1.2 fusion.6
  267.0 1.9 fusion.8
  268.9 41.3 %collective-permute-done.6 = f32[512,1152]{1,0:T(8,128)S(1)} collective-permute-done((f32[512,1152]{1,0:T(8,128)S(1)}, f32[512,1152]{1,0:T(8,128)S(1)}, u32[]{:S(2)}, u32[]{:S(2)}) %collective-permute-start.6) | collective-permute-done | bytes 2359328 | tf_op jit(solution)/shard_map/ppermute | solution.py:14
  310.7 1.9 fusion.12
  (17 shorter events, 3.4 us)
Async XLA Ops:
  0.6 3.9 %copy-start.1 = (bf16[512,1152]{1,0:T(8,128)(2,1)S(1)}, bf16[512,1152]{1,0:T(8,128)(2,1)}, u32[]{:S(2)}) copy-start(bf16[512,1152]{1,0:T(8,128)(2,1)} %param.4) | copy-start | bytes 3538948
  8.2 78.8 %collective-permute-start.3 = (f32[512,1152]{1,0:T(8,128)S(1)}, f32[512,1152]{1,0:T(8,128)S(1)}, u32[]{:S(2)}, u32[]{:S(2)}) collective-permute-start(f32[512,1152]{1,0:T(8,128)S(1)} %fusion.24), channel_id=1, source_target_pairs={{0,1},{1,2},{2,3},{3,4},{4,5},{5,6},{6,7},{7,8},{8,9},{9,10},{10,1... | collective-permute-start | bytes 7077896 | tf_op jit(solution)/shard_map/ppermute | solution.py:14
  9.7 75.8 %collective-permute-start = (bf16[512,1152]{1,0:T(8,128)(2,1)S(1)}, bf16[512,1152]{1,0:T(8,128)(2,1)S(1)}, u32[]{:S(2)}, u32[]{:S(2)}) collective-permute-start(bf16[512,1152]{1,0:T(8,128)(2,1)S(1)} %fusion.2), channel_id=1, source_target_pairs={{0,1},{1,2},{2,3},{3,4},{4,5},{5,6},{6,7},{7,8},{8,9},{9,10},{10,1... | collective-permute-start | bytes 3538952 | tf_op jit(solution)/shard_map/ppermute | solution.py:14
  88.1 81.6 %collective-permute-start.4 = (f32[512,1152]{1,0:T(8,128)S(1)}, f32[512,1152]{1,0:T(8,128)S(1)}, u32[]{:S(2)}, u32[]{:S(2)}) collective-permute-start(f32[512,1152]{1,0:T(8,128)S(1)} %convolution_add_fusion), channel_id=1, source_target_pairs={{0,1},{1,2},{2,3},{3,4},{4,5},{5,6},{6,7},{7,8},{8,9},{9,10},{10,1... | collective-permute-start | bytes 7077896 | tf_op jit(solution)/shard_map/ppermute | solution.py:14
  92.2 74.9 %collective-permute-start.1 = (bf16[512,1152]{1,0:T(8,128)(2,1)S(1)}, bf16[512,1152]{1,0:T(8,128)(2,1)S(1)}, u32[]{:S(2)}, u32[]{:S(2)}) collective-permute-start(bf16[512,1152]{1,0:T(8,128)(2,1)S(1)} %collective-permute-done), channel_id=1, source_target_pairs={{0,1},{1,2},{2,3},{3,4},{4,5},{5,6},{6,7},{7,8},{8,9},{9,10},{10,1... | collective-permute-start | bytes 3538952 | tf_op jit(solution)/shard_map/ppermute | solution.py:14
  169.9 82.0 %collective-permute-start.5 = (f32[512,1152]{1,0:T(8,128)S(1)}, f32[512,1152]{1,0:T(8,128)S(1)}, u32[]{:S(2)}, u32[]{:S(2)}) collective-permute-start(f32[512,1152]{1,0:T(8,128)S(1)} %add.110), channel_id=1, source_target_pairs={{0,1},{1,2},{2,3},{3,4},{4,5},{5,6},{6,7},{7,8},{8,9},{9,10},{10,1... | collective-permute-start | bytes 7077896 | tf_op jit(solution)/shard_map/ppermute | solution.py:14
  174.2 75.1 %collective-permute-start.2 = (bf16[512,1152]{1,0:T(8,128)(2,1)S(1)}, bf16[512,1152]{1,0:T(8,128)(2,1)S(1)}, u32[]{:S(2)}, u32[]{:S(2)}) collective-permute-start(bf16[512,1152]{1,0:T(8,128)(2,1)S(1)} %collective-permute-done.1), channel_id=1, source_target_pairs={{0,1},{1,2},{2,3},{3,4},{4,5},{5,6},{6,7},{7,8},{8,9},{9,10},{10,1... | collective-permute-start | bytes 3538952 | tf_op jit(solution)/shard_map/ppermute | solution.py:14
  252.2 58.1 %collective-permute-start.6 = (f32[512,1152]{1,0:T(8,128)S(1)}, f32[512,1152]{1,0:T(8,128)S(1)}, u32[]{:S(2)}, u32[]{:S(2)}) collective-permute-start(f32[512,1152]{1,0:T(8,128)S(1)} %add.111), channel_id=1, source_target_pairs={{0,253},{1,254},{2,255},{3,0},{4,1},{5,2},{6,3},{7,4},{8,5},{9,6},... | collective-permute-start | bytes 7077896 | tf_op jit(solution)/shard_map/ppermute | solution.py:14
  267.0 43.2 %copy-start = (bf16[512,1152]{1,0:T(8,128)(2,1)S(1)}, bf16[512,1152]{1,0:T(8,128)(2,1)}, u32[]{:S(2)}) copy-start(bf16[512,1152]{1,0:T(8,128)(2,1)} %param.5) | copy-start | bytes 3538948
where the time goes:
time: 314 us; the launch traced here: 313 us
  waiting for transfers between devices  264 us (84%)
  starting transfers between devices  22.8 us (7%)
  matrix products  14.4 us (5%)
  other arithmetic  8.7 us (3%)
    ppermute x7, waiting for transfers between devices, shifted(): return lax.ppermute(x, axis, [(i, (i + by) % count) for i in range(count)])  264 us
    ppermute x7, starting transfers between devices, shifted(): return lax.ppermute(x, axis, [(i, (i + by) % count) for i in range(count)])  22.8 us
  transfers between devices with their start and end apart: 7, of which 4 were waited for; matrix products, arithmetic and copies ran while one was open for 4% of the time, Pallas kernels for 0%

commit v1 on v0

v1 whole, which is shorter than its diff:
```python
import jax
import jax.numpy as jnp
from jax import lax
from jax.sharding import PartitionSpec as P

STEPS = 4

EPSILON = 1e-06


def shifted(x, axis, by):
    count = lax.axis_size(axis)
    return lax.ppermute(x, axis, [(i, (i + by) % count) for i in range(count)])


def unit_rows(embedding):
    values = embedding.astype(jnp.float32)
    scale = lax.rsqrt(jnp.sum(values * values, axis=-1, keepdims=True) + EPSILON)
    return (values * scale, scale)


def low_rows(embedding):
    return unit_rows(embedding)[0].astype(jnp.bfloat16)


def block_logits(image_low, text_low, temper, bias):
    product = lax.dot_general(
        image_low, text_low, (((1,), (1,)), ((), ())), preferred_element_type=jnp.float32
    )
    return temper * product + bias


def block_losses(logits, labels):
    return -jnp.sum(jax.nn.log_sigmoid(labels * logits), axis=-1)


def block_weights(logits, labels, temper):
    return (-labels * jax.nn.sigmoid(-labels * logits) * temper).astype(jnp.bfloat16)


def for_image(weights, text_low):
    return jnp.dot(weights, text_low, preferred_element_type=jnp.float32)


def for_text(weights, image_low):
    return lax.dot_general(
        weights, image_low, (((0,), (0,)), ((), ())), preferred_element_type=jnp.float32
    )


def unit_backward(unit, scale, grad_unit):
    return scale * (grad_unit - unit * jnp.sum(unit * grad_unit, axis=-1, keepdims=True))


def body(image_emb, text_emb, log_temp, bias):
    row_count = image_emb.shape[0]
    axes = ("blk", "rep")
    texts = [shifted(text_emb, axes, o) for o in range(1, STEPS)]
    images = [shifted(image_emb, axes, -o) for o in range(1, STEPS)]
    image_unit, image_scale = unit_rows(image_emb)
    text_unit, text_scale = unit_rows(text_emb)
    image_low = image_unit.astype(jnp.bfloat16)
    text_low = text_unit.astype(jnp.bfloat16)
    temper = jnp.exp(log_temp)
    positive = 2.0 * jnp.eye(row_count, dtype=jnp.float32) - 1.0
    negative = -jnp.ones((row_count, row_count), jnp.float32)
    logits = block_logits(image_low, text_low, temper, bias)
    losses = block_losses(logits, positive)
    weights = block_weights(logits, positive, temper)
    grad_img = for_image(weights, text_low)
    grad_txt = for_text(weights, image_low)
    for text, image in zip(texts, images):
        partner = low_rows(text)
        logits = block_logits(image_low, partner, temper, bias)
        losses = losses + block_losses(logits, negative)
        grad_img = grad_img + for_image(block_weights(logits, negative, temper), partner)
        partner = low_rows(image)
        logits = block_logits(partner, text_low, temper, bias)
        grad_txt = grad_txt + for_text(block_weights(logits, negative, temper), partner)
    grad_image = unit_backward(image_unit, image_scale, grad_img)
    grad_text = unit_backward(text_unit, text_scale, grad_txt)
    return (losses, grad_image, grad_text)


def solution(mesh):
    return jax.shard_map(
        body,
        mesh=mesh,
        in_specs=(P(("blk", "rep"), None), P(("blk", "rep"), None), P(), P()),
        out_specs=(P(("blk", "rep")), P(("blk", "rep"), None), P(("blk", "rep"), None)),
        check_vma=False,
    )
```

time: 314 us -> 150 us (0.48)
  the two profiles are of different devices: /device:TPU:0 before, /device:TPU:1 now
where the time goes in v1:
time: 150 us
  starting transfers between devices  59.9 us (40%)
  matrix products  34.3 us (23%)
  waiting for transfers between devices  33.6 us (22%)
  other arithmetic  19 us (13%)
  between operations  2.12 us (1%)
    ppermute x6, starting transfers between devices, shifted(): return lax.ppermute(x, axis, [(i, (i + by) % count) for i in range(count)])  59.9 us
    ppermute x6, waiting for transfers between devices, shifted(): return lax.ppermute(x, axis, [(i, (i + by) % count) for i in range(count)])  33.6 us
    dot_general x4, matrix products, for_text(): lax.dot_general(weights, image_low, (((0,), (0,)), ((), ())), preferred_e...  19.6 us
    reduce_sum x8, other arithmetic, unit_rows(): jnp.sum(values * values, axis=-1, keepdims=True) + EPSILON  10.1 us
    dot_general x4, matrix products, block_logits(): lax.dot_general(image_low, text_low, (((1,), (1,)), ((), ())), preferred_...  7.52 us
    dot_general x4, matrix products, for_image(): return jnp.dot(weights, text_low, preferred_element_type=jnp.float32)  7.23 us
    mul x2, other arithmetic, unit_backward(): scale * (grad_unit - unit * jnp.sum(unit * grad_unit, axis=-1, keepdims=T...  5.4 us
  transfers between devices with their start and end apart: 6, of which 2 were waited for; matrix products, arithmetic and copies ran while one was open for 12% of the time, Pallas kernels for 0%

profile of v1, /device:TPU:1, one launch (start us, length us, event | category | flops | bytes accessed | tf_op | source)
XLA Modules:
  0.0 150.0 jit_solution(16111465863364448696)
XLA Ops:
  0.7 4.4 %collective-permute-start.3 = (bf16[512,1152]{1,0:T(8,128)(2,1)}, bf16[512,1152]{1,0:T(8,128)(2,1)}, u32[]{:S(2)}, u32[]{:S(2)}) collective-permute-start(bf16[512,1152]{1,0:T(8,128)(2,1)} %param.4), channel_id=1, source_target_pairs={{0,255},{1,0},{2,1},{3,2},{4,3},{5,4},{6,5},{7,6},{8,7},{9,8},{10,... | collective-permute-start | bytes 3538952 | tf_op jit(solution)/shard_map/ppermute | solution.py:13
  5.0 7.7 %collective-permute-start.5 = (bf16[512,1152]{1,0:T(8,128)(2,1)}, bf16[512,1152]{1,0:T(8,128)(2,1)}, u32[]{:S(2)}, u32[]{:S(2)}) collective-permute-start(bf16[512,1152]{1,0:T(8,128)(2,1)} %param.4), channel_id=1, source_target_pairs={{0,253},{1,254},{2,255},{3,0},{4,1},{5,2},{6,3},{7,4},{8,5},{9,6},... | collective-permute-start | bytes 3538952 | tf_op jit(solution)/shard_map/ppermute | solution.py:13
  15.6 1.6 %fusion.11 = f32[512]{0:T(512)S(1)} fusion(bf16[512,1152]{1,0:T(8,128)(2,1)} %param.4), kind=kLoop, calls=%fused_computation.35 | loop fusion | flops 1768960 | bytes 1181696 | tf_op jit(solution)/shard_map/reduce_sum | solution.py:18
  17.2 1.6 %fusion.15 = f32[512]{0:T(512)S(1)} fusion(bf16[512,1152]{1,0:T(8,128)(2,1)} %param.5), kind=kLoop, calls=%fused_computation.39 | loop fusion | flops 1768960 | bytes 1181696 | tf_op jit(solution)/shard_map/reduce_sum | solution.py:18
  20.1 1.6 %fusion.58 = (f32[512]{0:T(512)S(1)}, f32[512,512]{0,1:T(8,128)S(1)}) fusion(f32[]{:T(128)S(6)} %copy.8, bf16[512,1152]{1,0:T(8,128)(2,1)S(1)} %copy-done, f32[512]{0:T(512)S(1)} %get-tuple-element.15, bf16[512,1152]{1,0:T(8,128)(2,1)S(1)} %copy-done.1, f32[512]{0:T(512)S(1)} %get-tuple-element.16, f32[]{:T(128)S(6)} %exp.38), kind=kOutput, calls=%fused_computation.86 | convolution fusion | flops 611188224 | bytes 3414024 | tf_op jit(solution)/shard_map/dot_general | solution.py:27
  21.7 2.5 %fusion.94 = f32[512,1152]{1,0:T(8,128)} fusion(f32[512,512]{0,1:T(8,128)S(1)} %get-tuple-element.8, f32[]{:T(128)S(6)} %exp.38, bf16[512,1152]{1,0:T(8,128)(2,1)S(1)} %copy-done.1, f32[512]{0:T(512)S(1)} %get-tuple-element.16), kind=kOutput, calls=%fused_computation.127 | convolution fusion | flops 608632832 | bytes 4589572 | tf_op jit(solution)/shard_map/dot_general | solution.py:46
  24.2 2.5 %fusion.95 = f32[512,1152]{1,0:T(8,128)} fusion(f32[512,512]{0,1:T(8,128)S(1)} %get-tuple-element.8, f32[]{:T(128)S(6)} %exp.38, bf16[512,1152]{1,0:T(8,128)(2,1)S(1)} %copy-done, f32[512]{0:T(512)S(1)} %get-tuple-element.15), kind=kOutput, calls=%fused_computation.128 | convolution fusion | flops 608632832 | bytes 4589572 | tf_op jit(solution)/shard_map/dot_general | solution.py:42
  26.7 21.9 %collective-permute-done.3 = bf16[512,1152]{1,0:T(8,128)(2,1)} collective-permute-done((bf16[512,1152]{1,0:T(8,128)(2,1)}, bf16[512,1152]{1,0:T(8,128)(2,1)}, u32[]{:S(2)}, u32[]{:S(2)}) %collective-permute-start.3) | collective-permute-done | bytes 1179680 | tf_op jit(solution)/shard_map/ppermute | solution.py:13
  48.6 45.0 %collective-permute-start.1 = (bf16[512,1152]{1,0:T(8,128)(2,1)S(1)}, bf16[512,1152]{1,0:T(8,128)(2,1)S(1)}, u32[]{:S(2)}, u32[]{:S(2)}) collective-permute-start(bf16[512,1152]{1,0:T(8,128)(2,1)S(1)} %copy-done), channel_id=1, source_target_pairs={{0,2},{1,3},{2,4},{3,5},{4,6},{5,7},{6,8},{7,9},{8,10},{9,11},{10,... | collective-permute-start | bytes 3538952 | tf_op jit(solution)/shard_map/ppermute | solution.py:13
  93.6 1.6 %fusion.22 = f32[512]{0:T(512)S(1)} fusion(bf16[512,1152]{1,0:T(8,128)(2,1)} %collective-permute-done.3), kind=kLoop, calls=%fused_computation.46 | loop fusion | flops 1768960 | bytes 1181696 | tf_op jit(solution)/shard_map/reduce_sum | solution.py:18
  95.2 11.7 %collective-permute-done.5 = bf16[512,1152]{1,0:T(8,128)(2,1)} collective-permute-done((bf16[512,1152]{1,0:T(8,128)(2,1)}, bf16[512,1152]{1,0:T(8,128)(2,1)}, u32[]{:S(2)}, u32[]{:S(2)}) %collective-permute-start.5) | collective-permute-done | bytes 1179680 | tf_op jit(solution)/shard_map/ppermute | solution.py:13
  106.9 1.6 %fusion.26 = f32[512]{0:T(512)S(1)} fusion(bf16[512,1152]{1,0:T(8,128)(2,1)} %collective-permute-done.5), kind=kLoop, calls=%fused_computation.50 | loop fusion | flops 1768960 | bytes 1181696 | tf_op jit(solution)/shard_map/reduce_sum | solution.py:18
  108.5 1.6 %fusion.24 = f32[512]{0:T(512)S(1)} fusion(bf16[512,1152]{1,0:T(8,128)(2,1)} %collective-permute-done.4), kind=kLoop, calls=%fused_computation.48 | loop fusion | flops 1768960 | bytes 1181696 | tf_op jit(solution)/shard_map/reduce_sum | solution.py:18
  110.3 1.6 %fusion.20 = f32[512]{0:T(512)S(1)} fusion(bf16[512,1152]{1,0:T(8,128)(2,1)} %collective-permute-done.2), kind=kLoop, calls=%fused_computation.44 | loop fusion | flops 1768960 | bytes 1181696 | tf_op jit(solution)/shard_map/reduce_sum | solution.py:18
  116.2 4.9 %fusion.53 = f32[512,1152]{1,0:T(8,128)} fusion(bf16[512,1152]{1,0:T(8,128)(2,1)} %collective-permute-done.5, f32[512]{0:T(512)} %add_rsqrt_fusion, f32[]{:T(128)S(6)} %copy.8, f32[]{:T(128)S(6)} %exp.38, bf16[512,1152]{1,0:T(8,128)(2,1)S(1)} %copy-done, f32[512]{0:T(512)S(1)} %get-tuple-element.15), kind=kOutput, calls=%fused_computation.84 | convolution fusion | flops 1215102976 | bytes 4722696 | tf_op jit(solution)/shard_map/dot_general | solution.py:46
  121.1 5.6 %convolution_add_fusion.1 = f32[512,1152]{1,0:T(8,128)} fusion(f32[512,1152]{1,0:T(8,128)} %fusion.94, bf16[512,1152]{1,0:T(8,128)(2,1)} %collective-permute-done.3, f32[512]{0:T(512)S(1)} %add_rsqrt_fusion.2, f32[]{:T(128)S(6)} %copy.8, f32[]{:T(128)S(6)} %exp.38, bf16[512,1152]{1,0:T(8,128)(2,1)S(1)} %copy-done, f32[512]{0:T(512)S(1)} %get-tuple-element.15), kind=kOutput, calls=%fused_computation.1 | convolution fusion | flops 1215692800 | bytes 7081992 | tf_op jit(solution)/shard_map/dot_general | solution.py:46
  126.7 6.5 %fusion.12 = (f32[512]{0:T(512)S(1)}, f32[512,1152]{1,0:T(8,128)}) fusion(bf16[512,1152]{1,0:T(8,128)(2,1)S(1)} %copy-done, f32[512]{0:T(512)S(1)} %get-tuple-element.15, f32[512,1152]{1,0:T(8,128)} %fusion.53, f32[512,1152]{1,0:T(8,128)} %convolution_add_fusion.1, bf16[512,1152]{1,0:T(8,128)(2,1)} %collective-permute-done.4, f32[512]{0:T(512)} %add_rsqrt_fusion.1, ...), kind=kOutput, calls=%fused_computation.36 | convolution fusion | flops 1218641408 | bytes 9443336 | tf_op jit(solution)/shard_map/dot_general | solution.py:46
  133.2 3.5 %fusion.14 = f32[512,1152]{1,0:T(8,128)} fusion(f32[512,1152]{1,0:T(8,128)} %get-tuple-element.14, bf16[512,1152]{1,0:T(8,128)(2,1)S(1)} %copy-done, f32[512]{0:T(512)S(1)} %get-tuple-element.13, f32[512]{0:T(512)S(1)} %get-tuple-element.15), kind=kLoop, calls=%fused_computation.38 | loop fusion | flops 2949120 | bytes 5902336 | tf_op jit(solution)/shard_map/mul | solution.py:52
  136.7 1.5 fusion.59
  138.2 2.8 %fusion.61 = (f32[512]{0:T(512)S(1)}, f32[512,512]{0,1:T(8,128)S(1)}) fusion(f32[]{:T(128)S(6)} %copy.8, bf16[512,1152]{1,0:T(8,128)(2,1)} %collective-permute-done.2, f32[512]{0:T(512)S(1)} %copy-done.6, bf16[512,1152]{1,0:T(8,128)(2,1)S(1)} %copy-done.1, f32[512]{0:T(512)S(1)} %get-tuple-element.16, f32[]{:T(128)S(6)} %exp.38), kind=kOutput, calls=%fused_computation.89 | convolution fusion | flops 610401792 | bytes 3414024 | tf_op jit(solution)/shard_map/dot_general | solution.py:27
  141.0 2.4 %fusion.66 = f32[512,1152]{1,0:T(8,128)S(1)} fusion(f32[512,512]{0,1:T(8,128)S(1)} %get-tuple-element.4, f32[]{:T(128)S(6)} %exp.38, bf16[512,1152]{1,0:T(8,128)(2,1)} %collective-permute-done.2, f32[512]{0:T(512)S(1)} %copy-done.6), kind=kOutput, calls=%fused_computation.96 | convolution fusion | flops 607059968 | bytes 4589572 | tf_op jit(solution)/shard_map/dot_general | solution.py:42
  143.4 1.7 %fusion.60 = (f32[512]{0:T(512)S(1)}, f32[512,512]{0,1:T(8,128)S(1)}) fusion(f32[]{:T(128)S(6)} %copy.8, bf16[512,1152]{1,0:T(8,128)(2,1)S(1)} %copy-done.3, f32[512]{0:T(512)S(1)} %copy-done.5, bf16[512,1152]{1,0:T(8,128)(2,1)S(1)} %copy-done.1, f32[512]{0:T(512)S(1)} %get-tuple-element.16, f32[]{:T(128)S(6)} %exp.38), kind=kOutput, calls=%fused_computation.88 | convolution fusion | flops 610401792 | bytes 3414024 | tf_op jit(solution)/shard_map/dot_general | solution.py:27
  146.2 1.3 fusion.8
  147.5 1.9 %fusion.10 = f32[512,1152]{1,0:T(8,128)} fusion(f32[512,1152]{1,0:T(8,128)S(1)} %get-tuple-element.12, bf16[512,1152]{1,0:T(8,128)(2,1)S(1)} %copy-done.1, f32[512]{0:T(512)S(1)} %get-tuple-element.11, f32[512]{0:T(512)S(1)} %get-tuple-element.16), kind=kLoop, calls=%fused_computation.34 | loop fusion | flops 2949120 | bytes 5902336 | tf_op jit(solution)/shard_map/mul | solution.py:52
  (34 shorter events, 9.1 us)
Async XLA Ops:
  0.6 19.5 %copy-start.1 = (bf16[512,1152]{1,0:T(8,128)(2,1)S(1)}, bf16[512,1152]{1,0:T(8,128)(2,1)}, u32[]{:S(2)}) copy-start(bf16[512,1152]{1,0:T(8,128)(2,1)} %param.4) | copy-start | bytes 3538948
  0.6 19.5 %copy-start = (bf16[512,1152]{1,0:T(8,128)(2,1)S(1)}, bf16[512,1152]{1,0:T(8,128)(2,1)}, u32[]{:S(2)}) copy-start(bf16[512,1152]{1,0:T(8,128)(2,1)} %param.5) | copy-start | bytes 3538948
  0.7 48.0 %collective-permute-start.3 = (bf16[512,1152]{1,0:T(8,128)(2,1)}, bf16[512,1152]{1,0:T(8,128)(2,1)}, u32[]{:S(2)}, u32[]{:S(2)}) collective-permute-start(bf16[512,1152]{1,0:T(8,128)(2,1)} %param.4), channel_id=1, source_target_pairs={{0,255},{1,0},{2,1},{3,2},{4,3},{5,4},{6,5},{7,6},{8,7},{9,8},{10,... | collective-permute-start | bytes 3538952 | tf_op jit(solution)/shard_map/ppermute | solution.py:13
  5.0 101.8 %collective-permute-start.5 = (bf16[512,1152]{1,0:T(8,128)(2,1)}, bf16[512,1152]{1,0:T(8,128)(2,1)}, u32[]{:S(2)}, u32[]{:S(2)}) collective-permute-start(bf16[512,1152]{1,0:T(8,128)(2,1)} %param.4), channel_id=1, source_target_pairs={{0,253},{1,254},{2,255},{3,0},{4,1},{5,2},{6,3},{7,4},{8,5},{9,6},... | collective-permute-start | bytes 3538952 | tf_op jit(solution)/shard_map/ppermute | solution.py:13
  12.7 95.7 %collective-permute-start.4 = (bf16[512,1152]{1,0:T(8,128)(2,1)}, bf16[512,1152]{1,0:T(8,128)(2,1)}, u32[]{:S(2)}, u32[]{:S(2)}) collective-permute-start(bf16[512,1152]{1,0:T(8,128)(2,1)} %param.4), channel_id=1, source_target_pairs={{0,254},{1,255},{2,0},{3,1},{4,2},{5,3},{6,4},{7,5},{8,6},{9,7},{1... | collective-permute-start | bytes 3538952 | tf_op jit(solution)/shard_map/ppermute | solution.py:13
  14.0 96.1 %collective-permute-start = (bf16[512,1152]{1,0:T(8,128)(2,1)}, bf16[512,1152]{1,0:T(8,128)(2,1)S(1)}, u32[]{:S(2)}, u32[]{:S(2)}) collective-permute-start(bf16[512,1152]{1,0:T(8,128)(2,1)} %param.5), channel_id=1, source_target_pairs={{0,1},{1,2},{2,3},{3,4},{4,5},{5,6},{6,7},{7,8},{8,9},{9,10},{10,1... | collective-permute-start | bytes 3538952 | tf_op jit(solution)/shard_map/ppermute | solution.py:13
  15.1 95.2 %collective-permute-start.2 = (bf16[512,1152]{1,0:T(8,128)(2,1)}, bf16[512,1152]{1,0:T(8,128)(2,1)}, u32[]{:S(2)}, u32[]{:S(2)}) collective-permute-start(bf16[512,1152]{1,0:T(8,128)(2,1)} %param.5), channel_id=1, source_target_pairs={{0,3},{1,4},{2,5},{3,6},{4,7},{5,8},{6,9},{7,10},{8,11},{9,12},{10... | collective-permute-start | bytes 3538952 | tf_op jit(solution)/shard_map/ppermute | solution.py:13
  48.6 65.6 %collective-permute-start.1 = (bf16[512,1152]{1,0:T(8,128)(2,1)S(1)}, bf16[512,1152]{1,0:T(8,128)(2,1)S(1)}, u32[]{:S(2)}, u32[]{:S(2)}) collective-permute-start(bf16[512,1152]{1,0:T(8,128)(2,1)S(1)} %copy-done), channel_id=1, source_target_pairs={{0,2},{1,3},{2,4},{3,5},{4,6},{5,7},{6,8},{7,9},{8,10},{9,11},{10,... | collective-permute-start | bytes 3538952 | tf_op jit(solution)/shard_map/ppermute | solution.py:13
  114.2 1.0 copy-start.2
  133.2 3.5 %copy-start.4 = (f32[512]{0:T(512)S(1)}, f32[512]{0:T(512)}, u32[]{:S(2)}) copy-start(f32[512]{0:T(512)} %add_rsqrt_fusion.5) | copy-start | bytes 6148
  136.7 1.5 copy-start.6
  141.0 2.4 %copy-start.3 = (bf16[512,1152]{1,0:T(8,128)(2,1)S(1)}, bf16[512,1152]{1,0:T(8,128)(2,1)}, u32[]{:S(2)}) copy-start(bf16[512,1152]{1,0:T(8,128)(2,1)} %copy-done.2) | copy-start | bytes 3538948
  141.0 2.4 %copy-start.5 = (f32[512]{0:T(512)S(1)}, f32[512]{0:T(512)}, u32[]{:S(2)}) copy-start(f32[512]{0:T(512)} %add_rsqrt_fusion.4) | copy-start | bytes 6148
  143.4 1.7 %copy-start.7 = (f32[512,1152]{1,0:T(8,128)S(1)}, f32[512,1152]{1,0:T(8,128)}, u32[]{:S(2)}) copy-start(f32[512,1152]{1,0:T(8,128)} %fusion.95) | copy-start | bytes 7077892

commit v2 on v1

v2 whole, which is shorter than its diff:
```python
import functools

import jax
import jax.numpy as jnp
from jax import lax
from jax.experimental import pallas as pl
from jax.experimental.pallas import tpu as pltpu
from jax.sharding import PartitionSpec as P

AXES = ("blk", "rep")
EPSILON = 1e-06
CHUNK = 256
LANES = 128


def by_role(steps):
    def pairs():
        count = lax.axis_size(AXES)
        return [(b, (b + steps[b % 8]) % count) for b in range(count) if b % 8 in steps]

    return pairs


SWAP = by_role({0: 2, 1: 2, 4: 2, 5: 2, 2: -2, 3: -2, 6: -2, 7: -2})
SECOND = by_role({0: -2, 1: -2, 4: -2, 5: -2, 2: 2, 3: 2, 6: 2, 7: 2})
OF_MAIN = by_role({1: -3, 5: -3, 2: 3, 6: 3, 0: -1, 4: -1, 3: 1, 7: 1})
OF_OTHER = by_role({1: 3, 5: 3, 2: -3, 6: -3, 0: 1, 4: 1, 3: -1, 7: -1})
ON_BY_TWO = by_role({0: -2, 4: -2, 3: 2, 7: 2})
ON_BY_ONE = by_role({0: -1, 4: -1, 3: 1, 7: 1})


def send(x, pairs):
    return lax.ppermute(x, AXES, pairs())


def together(*arrays):
    return lax.optimization_barrier(arrays)


def scale_of(values):
    return lax.rsqrt(jnp.sum(values * values, axis=-1, keepdims=True) + EPSILON)


def lower(raw_ref, low_ref):
    for at in range(0, raw_ref.shape[0], CHUNK):
        rows = pl.ds(at, CHUNK)
        values = raw_ref[rows, :].astype(jnp.float32)
        low_ref[rows, :] = (values * scale_of(values)).astype(jnp.bfloat16)


def terms(logits):
    shrunk = jnp.exp(-jnp.abs(logits))
    total = 1.0 + shrunk
    losses = jnp.maximum(logits, 0.0) + jnp.log(total)
    return losses, jnp.where(logits >= 0.0, 1.0, shrunk) / total


def folded(losses):
    out = losses[:, :LANES]
    for at in range(LANES, losses.shape[1], LANES):
        out = out + losses[:, at : at + LANES]
    return out


def product(left, right, left_dim, right_dim):
    return lax.dot_general(
        left, right, (((left_dim,), (right_dim,)), ((), ())), preferred_element_type=jnp.float32
    )


def pair(numbers_ref, own_ref, partner_ref, acc_ref, loss_ref, counts):
    temper, bias = numbers_ref[0], numbers_ref[1]
    for at in range(0, own_ref.shape[0], CHUNK):
        rows = pl.ds(at, CHUNK)
        logits = temper * product(own_ref[rows, :], partner_ref[...], 1, 1) + bias
        losses, chances = terms(logits)
        loss_ref[rows, :] += counts * folded(losses)
        weights = (chances * temper).astype(jnp.bfloat16)
        acc_ref[rows, :] += product(weights, partner_ref[...], 1, 0)


def finish(raw_ref, acc_ref, out_ref):
    for at in range(0, raw_ref.shape[0], CHUNK):
        rows = pl.ds(at, CHUNK)
        values = raw_ref[rows, :].astype(jnp.float32)
        scale = scale_of(values)
        unit = values * scale
        grad = acc_ref[rows, :]
        out_ref[rows, :] = scale * (grad - unit * jnp.sum(unit * grad, axis=-1, keepdims=True))


def own_pair(numbers_ref, image, text, image_low, text_low, image_acc, text_acc, loss_ref, weights_ref):
    temper, bias = numbers_ref[0], numbers_ref[1]
    lower(image, image_low)
    lower(text, text_low)
    count = image.shape[0]
    for at in range(0, count, CHUNK):
        rows = pl.ds(at, CHUNK)
        logits = temper * product(image_low[rows, :], text_low[...], 1, 1) + bias
        row = lax.broadcasted_iota(jnp.int32, (CHUNK, count), 0) + at
        column = lax.broadcasted_iota(jnp.int32, (CHUNK, count), 1)
        same = row == column
        losses, chances = terms(jnp.where(same, -logits, logits))
        loss_ref[rows, :] = folded(losses)
        weights = (jnp.where(same, -chances, chances) * temper).astype(jnp.bfloat16)
        weights_ref[rows, :] = weights
        image_acc[rows, :] = product(weights, text_low[...], 1, 0)
    text_acc[...] = product(weights_ref[...], image_low[...], 0, 0)


def first_kernel(
    role_ref, numbers_ref, main, other, swapped,
    main_low, other_low, main_acc, other_acc, loss_ref, weights_ref, low_ref,
):
    @pl.when(role_ref[0] == 0)
    def _():
        own_pair(numbers_ref, main, other, main_low, other_low, main_acc, other_acc, loss_ref, weights_ref)

    @pl.when(role_ref[0] == 1)
    def _():
        own_pair(numbers_ref, other, main, other_low, main_low, other_acc, main_acc, loss_ref, weights_ref)

    lower(swapped, low_ref)
    pair(numbers_ref, other_low, low_ref, other_acc, loss_ref, role_ref[0].astype(jnp.float32))


def lower_one_of(chosen, this_ref, that_ref, low_ref):
    @pl.when(chosen)
    def _():
        lower(this_ref, low_ref)

    @pl.when(jnp.logical_not(chosen))
    def _():
        lower(that_ref, low_ref)


def middle_kernel(
    role_ref, numbers_ref, main_low, second, of_main, of_other, main_in, loss_in, main_acc, loss_ref, low_ref
):
    on_main = (1 - role_ref[0]).astype(jnp.float32)
    main_acc[...] = main_in[...]
    loss_ref[...] = loss_in[...]
    for partner in (second, of_main, of_other):
        lower(partner, low_ref)
        pair(numbers_ref, main_low, low_ref, main_acc, loss_ref, on_main)


def put(role_ref, main_side, value_ref, image_out, text_out, sem):
    to_image = role_ref[0] == (0 if main_side else 1)

    @pl.when(to_image)
    def _():
        copy = pltpu.make_async_copy(value_ref, image_out, sem)
        copy.start()
        copy.wait()

    @pl.when(jnp.logical_not(to_image))
    def _():
        copy = pltpu.make_async_copy(value_ref, text_out, sem)
        copy.start()
        copy.wait()


def shared_kernel(
    role_ref, numbers_ref, raw, other_low, swapped, main_in, other_in, loss_in,
    image_out, text_out, other_acc, loss_ref, low_ref, main_acc, sem,
):
    other_acc[...] = other_in[...]
    loss_ref[...] = loss_in[...]
    lower(swapped, low_ref)
    pair(numbers_ref, other_low, low_ref, other_acc, loss_ref, role_ref[0].astype(jnp.float32))
    main_acc[...] = main_in[...]
    finish(raw, main_acc, main_acc)
    put(role_ref, True, main_acc, image_out, text_out, sem)


def last_kernel(
    role_ref, numbers_ref, raw, other_low, by_one, by_two, other_in, loss_in, image_in, text_in,
    image_out, text_out, row_loss, low_ref, other_acc, loss_ref, sem,
):
    on_other = role_ref[0].astype(jnp.float32)
    other_acc[...] = other_in[...]
    loss_ref[...] = loss_in[...]
    lower_one_of(role_ref[0] == role_ref[1], by_one, by_two, low_ref)
    pair(numbers_ref, other_low, low_ref, other_acc, loss_ref, on_other)
    finish(raw, other_acc, other_acc)
    row_loss[...] = jnp.sum(loss_ref[...].T, axis=0, keepdims=True)
    put(role_ref, False, other_acc, image_out, text_out, sem)


def call(kernel, in_kinds, outs, scratch, aliases=None):
    kinds = {
        "s": pl.BlockSpec(memory_space=pltpu.SMEM),
        "v": pl.BlockSpec(memory_space=pltpu.VMEM),
        "a": pl.BlockSpec(memory_space=pl.ANY),
    }
    return pl.pallas_call(
        kernel,
        in_specs=[kinds[k] for k in in_kinds],
        out_specs=[kinds[k] for k, _, _ in outs],
        out_shape=[jax.ShapeDtypeStruct(shape, dtype) for _, shape, dtype in outs],
        scratch_shapes=scratch,
        input_output_aliases=aliases or {},
        compiler_params=pltpu.CompilerParams(vmem_limit_bytes=24 * 1024 * 1024),
    )


def body(image_emb, text_emb, log_temp, bias):
    rows, width = image_emb.shape
    place = lax.axis_index(AXES)
    core = (place // 2) % 2
    role = jnp.stack([core, place % 2]).astype(jnp.int32)
    numbers = jnp.stack([jnp.exp(log_temp), bias])
    is_core_1 = core == 1
    both_or_none = core == place % 2
    main = jnp.where(is_core_1, text_emb, image_emb)
    other = jnp.where(is_core_1, image_emb, text_emb)
    main, other = together(main, other)

    of_other = send(other, OF_OTHER)
    second = send(main, SECOND)
    of_main = send(main, OF_MAIN)
    swapped = send(other, SWAP)

    f32, low = jnp.float32, jnp.bfloat16
    whole, partial = (rows, width), (rows, LANES)
    main_low, other_low, main_acc, other_acc, loss = call(
        first_kernel,
        "ssvvv",
        [("v", whole, low), ("v", whole, low), ("v", whole, f32), ("v", whole, f32), ("v", partial, f32)],
        [pltpu.VMEM((rows, rows), low), pltpu.VMEM(whole, low)],
    )(role, numbers, main, other, swapped)

    of_other, second, of_main, loss = together(of_other, second, of_main, loss)
    by_two = send(of_other, ON_BY_TWO)
    by_one = send(second, ON_BY_ONE)
    swapped = send(jnp.where(both_or_none, of_main, of_other), SWAP)

    main_acc, loss = call(
        middle_kernel,
        "ssvvvvvv",
        [("v", whole, f32), ("v", partial, f32)],
        [pltpu.VMEM(whole, low)],
        {6: 0, 7: 1},
    )(role, numbers, main_low, second, of_main, of_other, main_acc, loss)

    grad_image, grad_text, other_acc, loss = call(
        shared_kernel,
        "ssvvvvvv",
        [("a", whole, f32), ("a", whole, f32), ("v", whole, f32), ("v", partial, f32)],
        [pltpu.VMEM(whole, low), pltpu.VMEM(whole, f32), pltpu.SemaphoreType.DMA],
        {6: 2, 7: 3},
    )(role, numbers, main, other_low, swapped, main_acc, other_acc, loss)

    grad_image, grad_text, row_loss = call(
        last_kernel,
        "ssvvvvvvaa",
        [("a", whole, f32), ("a", whole, f32), ("v", (1, rows), f32)],
        [pltpu.VMEM(whole, low), pltpu.VMEM(whole, f32), pltpu.VMEM(partial, f32), pltpu.SemaphoreType.DMA],
        {8: 0, 9: 1},
    )(role, numbers, other, other_low, by_one, by_two, other_acc, loss, grad_image, grad_text)
    return (row_loss.reshape(rows), grad_image, grad_text)


def solution(mesh):
    return jax.shard_map(
        body,
        mesh=mesh,
        in_specs=(P(AXES, None), P(AXES, None), P(), P()),
        out_specs=(P(AXES), P(AXES, None), P(AXES, None)),
        check_vma=False,
    )
```

time: 150 us -> 102 us (0.68)
  the two profiles are of different devices: /device:TPU:1 before, /device:TPU:0 now
where the time goes in v2:
time: 102 us; the launch traced here: 101 us
  waiting for transfers between devices  47.8 us (47%)
  Pallas kernels  26.5 us (26%)
  starting transfers between devices  21.4 us (21%)
  other arithmetic  3.4 us (3%)
  between operations  2.24 us (2%)
    ppermute x7, waiting for transfers between devices, send(): return lax.ppermute(x, AXES, pairs())  47.8 us
    ppermute x7, starting transfers between devices, send(): return lax.ppermute(x, AXES, pairs())  21.4 us
    pallas_call x1, Pallas kernels, body(): call(middle_kernel, 'ssvvvvvv', [('v', whole, f32), ('v', partial, f32)],...  8.63 us
    pallas_call x1, Pallas kernels, body(): call(first_kernel, 'ssvvv', [('v', whole, low), ('v', whole, low), ('v',...  7.14 us
    pallas_call x1, Pallas kernels, body(): call(last_kernel, 'ssvvvvvvaa', [('a', whole, f32), ('a', whole, f32), ('...  5.67 us
    pallas_call x1, Pallas kernels, body(): call(shared_kernel, 'ssvvvvvv', [('a', whole, f32), ('a', whole, f32), ('...  5.11 us
  transfers between devices with their start and end apart: 7, of which 4 were waited for; matrix products, arithmetic and copies ran while one was open for 0% of the time, Pallas kernels for 21%

profile of v2, /device:TPU:0, one launch (start us, length us, event | category | flops | bytes accessed | tf_op | source)
XLA Modules:
  0.0 101.4 jit_solution(7649345860621905302)
XLA Ops:
  0.7 1.8 %broadcast_select_fusion.1 = (bf16[512,1152]{1,0:T(8,128)(2,1)S(1)}, bf16[512,1152]{1,0:T(8,128)(2,1)S(1)}) fusion(bf16[512,1152]{1,0:T(8,128)(2,1)} %param.4, bf16[512,1152]{1,0:T(8,128)(2,1)} %param.5, pred[]{:T(512)S(6)} %eq.10), kind=kLoop, calls=%fused_computation.1 | loop fusion | flops 1179648 | bytes 4718593 | tf_op jit(solution)/shard_map/jit(_where)/select_n | solution.py:217
  2.5 0.1 collective-permute-start
  2.6 1.5 %collective-permute-start.1 = (bf16[512,1152]{1,0:T(8,128)(2,1)S(1)}, bf16[512,1152]{1,0:T(8,128)(2,1)S(1)}, u32[]{:S(2)}, u32[]{:S(2)}) collective-permute-start(bf16[512,1152]{1,0:T(8,128)(2,1)S(1)} %get-tuple-element.23.other.raw), channel_id=1, source_target_pairs={{0,1},{1,4},{2,255},{3,2},{4,5},{5,8},{6,3},{7,6},{8,9},{9,12},{10... | collective-permute-start | bytes 3538952 | tf_op jit(solution)/shard_map/ppermute | solution.py:33
  4.1 8.3 %collective-permute-start.3 = (bf16[512,1152]{1,0:T(8,128)(2,1)S(1)}, bf16[512,1152]{1,0:T(8,128)(2,1)}, u32[]{:S(2)}, u32[]{:S(2)}) collective-permute-start(bf16[512,1152]{1,0:T(8,128)(2,1)S(1)} %get-tuple-element.24.main.raw), channel_id=1, source_target_pairs={{0,255},{1,254},{2,5},{3,4},{4,3},{5,2},{6,9},{7,8},{8,7},{9,6},{1... | collective-permute-start | bytes 3538952 | tf_op jit(solution)/shard_map/ppermute | solution.py:33
  12.4 0.0 collective-permute-start.2
  13.8 0.1 pad_maximum_fusion.numbers_ref
  13.9 0.1 pad_add_fusion.role_ref
  13.9 0.0 collective-permute-done.swapped
  13.9 7.1 %shard_map.67 = (bf16[512,1152]{1,0:T(8,128)(2,1)S(1)}, bf16[512,1152]{1,0:T(8,128)(2,1)S(1)}, f32[512,1152]{1,0:T(8,128)S(1)}, f32[512,1152]{1,0:T(8,128)S(1)}, f32[512,128]{1,0:T(8,128)S(1)}) custom-call(s32[2]{0:T(128)S(1)} %pad_add_fusion.role_ref, f32[2]{0:T(128)S(1)} %pad_maximum_fusion.numbers_ref, bf16[512,1152]{1,0:T(8,128)(2,1)S(1)} %get-tuple-element.24.main.raw, ...), custom_call_target="tpu_custom_call" | custom-call | tf_op jit(solution)/shard_map/pallas_call | solution.py:227
  21.1 23.5 %collective-permute-done.1.of_other = bf16[512,1152]{1,0:T(8,128)(2,1)S(1)} collective-permute-done((bf16[512,1152]{1,0:T(8,128)(2,1)S(1)}, bf16[512,1152]{1,0:T(8,128)(2,1)S(1)}, u32[]{:S(2)}, u32[]{:S(2)}) %collective-permute-start.1) | collective-permute-done | bytes 1179680 | tf_op jit(solution)/shard_map/ppermute | solution.py:33
  44.6 0.7 collective-permute-done.3.of_main
  45.3 12.3 %collective-permute-done.2.second = bf16[512,1152]{1,0:T(8,128)(2,1)} collective-permute-done((bf16[512,1152]{1,0:T(8,128)(2,1)S(1)}, bf16[512,1152]{1,0:T(8,128)(2,1)}, u32[]{:S(2)}, u32[]{:S(2)}) %collective-permute-start.2) | collective-permute-done | bytes 1179680 | tf_op jit(solution)/shard_map/ppermute | solution.py:33
  57.6 1.4 %broadcast_select_fusion = bf16[512,1152]{1,0:T(8,128)(2,1)S(1)} fusion(bf16[512,1152]{1,0:T(8,128)(2,1)} %collective-permute-done.3.of_main, bf16[512,1152]{1,0:T(8,128)(2,1)S(1)} %collective-permute-done.1.of_other, pred[]{:T(512)S(6)} %eq.11), kind=kLoop, calls=%fused_computation | loop fusion | flops 589824 | bytes 3538945 | tf_op jit(solution)/shard_map/jit(_where)/select_n | solution.py:237
  59.1 0.1 collective-permute-start.6
  59.2 9.9 %collective-permute-start.4 = (bf16[512,1152]{1,0:T(8,128)(2,1)}, bf16[512,1152]{1,0:T(8,128)(2,1)S(1)}, u32[]{:S(2)}, u32[]{:S(2)}) collective-permute-start(bf16[512,1152]{1,0:T(8,128)(2,1)} %collective-permute-done.2.second), channel_id=1, source_target_pairs={{0,255},{3,4},{4,3},{7,8},{8,7},{11,12},{12,11},{15,16},{16,15},{1... | collective-permute-start | bytes 3538952 | tf_op jit(solution)/shard_map/ppermute | solution.py:33
  69.0 1.5 %collective-permute-start.5 = (bf16[512,1152]{1,0:T(8,128)(2,1)S(1)}, bf16[512,1152]{1,0:T(8,128)(2,1)S(1)}, u32[]{:S(2)}, u32[]{:S(2)}) collective-permute-start(bf16[512,1152]{1,0:T(8,128)(2,1)S(1)} %collective-permute-done.1.of_other), channel_id=1, source_target_pairs={{0,254},{3,5},{4,2},{7,9},{8,6},{11,13},{12,10},{15,17},{16,14},{1... | collective-permute-start | bytes 3538952 | tf_op jit(solution)/shard_map/ppermute | solution.py:33
  70.6 8.6 %shard_map.68 = (f32[512,1152]{1,0:T(8,128)S(1)}, f32[512,128]{1,0:T(8,128)S(1)}) custom-call(s32[2]{0:T(128)S(1)} %pad_add_fusion.role_ref, f32[2]{0:T(128)S(1)} %pad_maximum_fusion.numbers_ref, bf16[512,1152]{1,0:T(8,128)(2,1)S(1)} %get-tuple-element.30.main_low, ...), custom_call_target="tpu_custom_call", output_to_operand_aliasing={{0}: (6, {}), {1}: (7, {})} | custom-call | tf_op jit(solution)/shard_map/pallas_call | solution.py:239
  79.2 0.0 collective-permute-done.6.swapped
  79.2 5.1 %shard_map.69 = (f32[512,1152]{1,0:T(8,128)}, f32[512,1152]{1,0:T(8,128)}, f32[512,1152]{1,0:T(8,128)S(1)}, f32[512,128]{1,0:T(8,128)S(1)}) custom-call(s32[2]{0:T(128)S(1)} %pad_add_fusion.role_ref, f32[2]{0:T(128)S(1)} %pad_maximum_fusion.numbers_ref, ...), custom_call_target="tpu_custom_call", output_to_operand_aliasing={{2}: (6, {}), {3}: (7, {})} | custom-call | tf_op jit(solution)/shard_map/pallas_call | solution.py:247
  84.4 0.0 collective-permute-done.4.by_one
  84.4 11.2 %collective-permute-done.5.by_two = bf16[512,1152]{1,0:T(8,128)(2,1)S(1)} collective-permute-done((bf16[512,1152]{1,0:T(8,128)(2,1)S(1)}, bf16[512,1152]{1,0:T(8,128)(2,1)S(1)}, u32[]{:S(2)}, u32[]{:S(2)}) %collective-permute-start.5) | collective-permute-done | bytes 1179680 | tf_op jit(solution)/shard_map/ppermute | solution.py:33
  95.6 5.7 %shard_map.70 = (f32[512,1152]{1,0:T(8,128)}, f32[512,1152]{1,0:T(8,128)}, f32[1,512]{1,0:T(1,128)}) custom-call(s32[2]{0:T(128)S(1)} %pad_add_fusion.role_ref, f32[2]{0:T(128)S(1)} %pad_maximum_fusion.numbers_ref, bf16[512,1152]{1,0:T(8,128)(2,1)S(1)} %get-tuple-element.23.other.raw, ...), custom_call_target="tpu_custom_call", output_to_operand_aliasing={{0}: (8, {}), {1}: (9, {})} | custom-call | tf_op jit(solution)/shard_map/pallas_call | solution.py:255
Async XLA Ops:
  2.5 11.4 %collective-permute-start = (bf16[512,1152]{1,0:T(8,128)(2,1)S(1)}, bf16[512,1152]{1,0:T(8,128)(2,1)}, u32[]{:S(2)}, u32[]{:S(2)}) collective-permute-start(bf16[512,1152]{1,0:T(8,128)(2,1)S(1)} %get-tuple-element.23.other.raw), channel_id=1, source_target_pairs={{0,2},{1,3},{2,0},{3,1},{4,6},{5,7},{6,4},{7,5},{8,10},{9,11},{10,... | collective-permute-start | bytes 3538952 | tf_op jit(solution)/shard_map/ppermute | solution.py:33
  2.6 42.0 %collective-permute-start.1 = (bf16[512,1152]{1,0:T(8,128)(2,1)S(1)}, bf16[512,1152]{1,0:T(8,128)(2,1)S(1)}, u32[]{:S(2)}, u32[]{:S(2)}) collective-permute-start(bf16[512,1152]{1,0:T(8,128)(2,1)S(1)} %get-tuple-element.23.other.raw), channel_id=1, source_target_pairs={{0,1},{1,4},{2,255},{3,2},{4,5},{5,8},{6,3},{7,6},{8,9},{9,12},{10... | collective-permute-start | bytes 3538952 | tf_op jit(solution)/shard_map/ppermute | solution.py:33
  4.1 41.2 %collective-permute-start.3 = (bf16[512,1152]{1,0:T(8,128)(2,1)S(1)}, bf16[512,1152]{1,0:T(8,128)(2,1)}, u32[]{:S(2)}, u32[]{:S(2)}) collective-permute-start(bf16[512,1152]{1,0:T(8,128)(2,1)S(1)} %get-tuple-element.24.main.raw), channel_id=1, source_target_pairs={{0,255},{1,254},{2,5},{3,4},{4,3},{5,2},{6,9},{7,8},{8,7},{9,6},{1... | collective-permute-start | bytes 3538952 | tf_op jit(solution)/shard_map/ppermute | solution.py:33
  12.4 45.2 %collective-permute-start.2 = (bf16[512,1152]{1,0:T(8,128)(2,1)S(1)}, bf16[512,1152]{1,0:T(8,128)(2,1)}, u32[]{:S(2)}, u32[]{:S(2)}) collective-permute-start(bf16[512,1152]{1,0:T(8,128)(2,1)S(1)} %get-tuple-element.24.main.raw), channel_id=1, source_target_pairs={{0,254},{1,255},{2,4},{3,5},{4,2},{5,3},{6,8},{7,9},{8,6},{9,7},{1... | collective-permute-start | bytes 3538952 | tf_op jit(solution)/shard_map/ppermute | solution.py:33
  59.1 20.2 %collective-permute-start.6 = (bf16[512,1152]{1,0:T(8,128)(2,1)S(1)}, bf16[512,1152]{1,0:T(8,128)(2,1)S(1)}, u32[]{:S(2)}, u32[]{:S(2)}) collective-permute-start(bf16[512,1152]{1,0:T(8,128)(2,1)S(1)} %broadcast_select_fusion), channel_id=1, source_target_pairs={{0,2},{1,3},{2,0},{3,1},{4,6},{5,7},{6,4},{7,5},{8,10},{9,11},{10,... | collective-permute-start | bytes 3538952 | tf_op jit(solution)/shard_map/ppermute | solution.py:33
  59.2 25.2 %collective-permute-start.4 = (bf16[512,1152]{1,0:T(8,128)(2,1)}, bf16[512,1152]{1,0:T(8,128)(2,1)S(1)}, u32[]{:S(2)}, u32[]{:S(2)}) collective-permute-start(bf16[512,1152]{1,0:T(8,128)(2,1)} %collective-permute-done.2.second), channel_id=1, source_target_pairs={{0,255},{3,4},{4,3},{7,8},{8,7},{11,12},{12,11},{15,16},{16,15},{1... | collective-permute-start | bytes 3538952 | tf_op jit(solution)/shard_map/ppermute | solution.py:33
  69.0 26.6 %collective-permute-start.5 = (bf16[512,1152]{1,0:T(8,128)(2,1)S(1)}, bf16[512,1152]{1,0:T(8,128)(2,1)S(1)}, u32[]{:S(2)}, u32[]{:S(2)}) collective-permute-start(bf16[512,1152]{1,0:T(8,128)(2,1)S(1)} %collective-permute-done.1.of_other), channel_id=1, source_target_pairs={{0,254},{3,5},{4,2},{7,9},{8,6},{11,13},{12,10},{15,17},{16,14},{1... | collective-permute-start | bytes 3538952 | tf_op jit(solution)/shard_map/ppermute | solution.py:33
